TPU v7x, 32 devices: a whole 2x2x4 slice. The times are simulated.
32 devices in a mesh: seq: 16 (over z, y, core), rep: 2 (over x).
Axes of the slice: x: 2, y: 2, z: 4, core: 2. Of those that a mesh axis runs over, the one named last changes fastest.
Arguments:
- queries: bfloat16 [4096, 2048], P(('seq', 'rep')), may hold values from -128 to 128
- key_rows: bfloat16 [4096, 2048], P(('seq', 'rep')), may hold values from -4.5 to 4.5
- value_rows: bfloat16 [4096, 2048], P(('seq', 'rep')), may hold values from -6 to 6
- saved_output: bfloat16 [4096, 2048], P(('seq', 'rep')), may hold values from -6 to 6
- grad_output: bfloat16 [4096, 2048], P(('seq', 'rep')), may hold values from -6 to 6
- doc_lengths: int32 [16], replicated, may hold values from 1 to 1536, 4096 in all
Outputs:
- grad_query: bfloat16 [4096, 2048], P(('seq', 'rep'))
- grad_key: bfloat16 [4096, 2048], P(('seq', 'rep'))
- grad_value: bfloat16 [4096, 2048], P(('seq', 'rep'))
Inputs may be any that keep to these rules, and one draw needn't show every extreme that they name: `doc_lengths`: documents in sequence order; they sum to 4096 and the longest has exactly 1536 tokens.
All inputs are finite; a program needn't handle non-finite values.
Results may differ from a plain program's by a relative error of at most 0.014.
Values may be sent and summed in bfloat16 or wider, within the bound.
A program may use at most 128 MiB of HBM per device.

v0:
```python
import jax
import jax.numpy as jnp
from jax import lax
from jax.sharding import PartitionSpec as P

HEAD_DIM = 128
TILE = 512
BAND = 512


NEG_FILL = -1e30


def shifted(array, axis, by):
    length = lax.axis_size(axis)
    pairs = [(i, i + by) for i in range(length) if 0 <= i + by < length]
    return lax.ppermute(array, axis, pairs)


def tile_grads(
    tile_id,
    query_buf,
    query_base,
    key_buf,
    value_buf,
    key_base,
    output_buf,
    dout_buf,
    doc_ends,
    doc_lengths,
    grad_bufs,
):
    softmax_scale = HEAD_DIM ** (-0.5)
    row0 = tile_id * TILE
    row_ids = row0 + lax.iota(jnp.int32, TILE)
    query_tile = lax.dynamic_slice_in_dim(query_buf, row0 - query_base, TILE, 0)
    output_tile = lax.dynamic_slice_in_dim(output_buf, row0 - query_base, TILE, 0)
    dout_tile = lax.dynamic_slice_in_dim(dout_buf, row0 - query_base, TILE, 0)
    before = jnp.sum(
        jnp.where(doc_ends[None, :] <= row_ids[:, None], doc_lengths[None, :], 0), axis=1
    )
    low_key = jnp.minimum(before, row_ids - BAND + 1)
    first_block = jnp.maximum(low_key[0], 0) // TILE
    end_block = tile_id + 1

    def scores_of(block_id):
        col_ids = block_id * TILE + lax.iota(jnp.int32, TILE)
        key_tile = lax.dynamic_slice_in_dim(key_buf, block_id * TILE - key_base, TILE, 0)
        scores = (
            lax.dot_general(
                query_tile, key_tile, (((1,), (1,)), ((), ())), preferred_element_type=jnp.float32
            )
            * softmax_scale
        )
        allowed = (col_ids[None, :] <= row_ids[:, None]) & (col_ids[None, :] >= low_key[:, None])
        return (scores, allowed, key_tile)

    def stat_step(block_id, loop_state):
        row_max, row_sum = loop_state
        scores, allowed, unused = scores_of(block_id)
        masked = jnp.where(allowed, scores, NEG_FILL)
        new_max = jnp.maximum(row_max, jnp.max(masked, axis=1))
        fresh = jnp.sum(jnp.where(allowed, jnp.exp(masked - new_max[:, None]), 0.0), axis=1)
        return (new_max, row_sum * jnp.exp(row_max - new_max) + fresh)

    start_stats = (jnp.full((TILE,), NEG_FILL, jnp.float32), jnp.zeros((TILE,), jnp.float32))
    row_max, row_sum = lax.fori_loop(first_block, end_block, stat_step, start_stats)
    log_norm = row_max + jnp.log(row_sum)
    row_delta = jnp.sum(dout_tile.astype(jnp.float32) * output_tile.astype(jnp.float32), axis=1)

    def grad_step(block_id, loop_state):
        dq_tile, dk_buf, dv_buf = loop_state
        scores, allowed, key_tile = scores_of(block_id)
        offset = block_id * TILE - key_base
        value_tile = lax.dynamic_slice_in_dim(value_buf, offset, TILE, 0)
        weights = jnp.where(allowed, jnp.exp(scores - log_norm[:, None]), 0.0)
        weights_low = weights.astype(jnp.bfloat16)
        grad_weights = lax.dot_general(
            dout_tile, value_tile, (((1,), (1,)), ((), ())), preferred_element_type=jnp.float32
        )
        dscore = (weights * (grad_weights - row_delta[:, None])).astype(jnp.bfloat16)
        dq_tile = dq_tile + jnp.dot(dscore, key_tile, preferred_element_type=jnp.float32)
        dk_add = lax.dot_general(
            dscore, query_tile, (((0,), (0,)), ((), ())), preferred_element_type=jnp.float32
        )
        dv_add = lax.dot_general(
            weights_low, dout_tile, (((0,), (0,)), ((), ())), preferred_element_type=jnp.float32
        )
        dk_buf = lax.dynamic_update_slice_in_dim(
            dk_buf, lax.dynamic_slice_in_dim(dk_buf, offset, TILE, 0) + dk_add, offset, 0
        )
        dv_buf = lax.dynamic_update_slice_in_dim(
            dv_buf, lax.dynamic_slice_in_dim(dv_buf, offset, TILE, 0) + dv_add, offset, 0
        )
        return (dq_tile, dk_buf, dv_buf)

    dq_buf, dk_buf, dv_buf = grad_bufs
    start_grads = (jnp.zeros((TILE, query_buf.shape[1]), jnp.float32), dk_buf, dv_buf)
    dq_tile, dk_buf, dv_buf = lax.fori_loop(first_block, end_block, grad_step, start_grads)
    dq_buf = lax.dynamic_update_slice_in_dim(dq_buf, dq_tile, row0 - query_base, 0)
    return (dq_buf, dk_buf, dv_buf)


def shards(queries, key_rows, value_rows, saved_output, grad_output, doc_lengths):
    groups = lax.axis_size("seq")
    helpers = lax.axis_size("rep")
    helper = lax.axis_index("rep")
    tok_dev = queries.shape[0]
    span = tok_dev * groups
    tiles = span // TILE
    doc_ends = jnp.cumsum(doc_lengths)

    def split_heads(array):
        return array.reshape(1, 1, tok_dev, groups, -1)

    arrived = (
        lax.all_to_all(
            lax.all_to_all(split_heads(queries), "seq", split_axis=3, concat_axis=0, tiled=True),
            "rep",
            split_axis=0,
            concat_axis=1,
            tiled=True,
        ),
        lax.all_to_all(
            lax.all_to_all(split_heads(key_rows), "seq", split_axis=3, concat_axis=0, tiled=True),
            "rep",
            split_axis=0,
            concat_axis=1,
            tiled=True,
        ),
        lax.all_to_all(
            lax.all_to_all(split_heads(value_rows), "seq", split_axis=3, concat_axis=0, tiled=True),
            "rep",
            split_axis=0,
            concat_axis=1,
            tiled=True,
        ),
        lax.all_to_all(
            lax.all_to_all(
                split_heads(saved_output), "seq", split_axis=3, concat_axis=0, tiled=True
            ),
            "rep",
            split_axis=0,
            concat_axis=1,
            tiled=True,
        ),
        lax.all_to_all(
            lax.all_to_all(
                split_heads(grad_output), "seq", split_axis=3, concat_axis=0, tiled=True
            ),
            "rep",
            split_axis=0,
            concat_axis=1,
            tiled=True,
        ),
    )
    query_q, key_q, value_q, output_q, dout_q = [part.reshape(span, -1) for part in arrived]
    head_width = query_q.shape[1]
    reach = span - TILE
    prior_key, prior_value = shifted((key_q[TILE:], value_q[TILE:]), "rep", 1)
    key_buf = jnp.concatenate([prior_key, key_q], axis=0)
    value_buf = jnp.concatenate([prior_value, value_q], axis=0)
    start_row = helper * span
    key_base = start_row - reach

    def visit(step_id, grad_bufs):
        return tile_grads(
            helper * tiles + step_id,
            query_q,
            start_row,
            key_buf,
            value_buf,
            key_base,
            output_q,
            dout_q,
            doc_ends,
            doc_lengths,
            grad_bufs,
        )

    start_bufs = (
        jnp.zeros((span, head_width), jnp.float32),
        jnp.zeros((span + reach, head_width), jnp.float32),
        jnp.zeros((span + reach, head_width), jnp.float32),
    )
    dq_own, dk_buf, dv_buf = lax.fori_loop(0, tiles, visit, start_bufs)
    spill_key, spill_value = (
        shifted(dk_buf[:reach].astype(jnp.bfloat16), "rep", -1).astype(jnp.float32),
        shifted(dv_buf[:reach].astype(jnp.bfloat16), "rep", -1).astype(jnp.float32),
    )
    dk_own = dk_buf[reach:] + jnp.pad(spill_key, ((TILE, 0), (0, 0)))
    dv_own = dv_buf[reach:] + jnp.pad(spill_value, ((TILE, 0), (0, 0)))
    softmax_scale = HEAD_DIM ** (-0.5)

    def to_tokens(grad, factor):
        return (
            (grad * factor).astype(jnp.bfloat16).reshape(groups // helpers, helpers, tok_dev, 1, -1)
        )

    home_query, home_key, home_value = (
        lax.all_to_all(
            to_tokens(dq_own, softmax_scale), "rep", split_axis=1, concat_axis=0, tiled=True
        ),
        lax.all_to_all(
            to_tokens(dk_own, softmax_scale), "rep", split_axis=1, concat_axis=0, tiled=True
        ),
        lax.all_to_all(to_tokens(dv_own, 1.0), "rep", split_axis=1, concat_axis=0, tiled=True),
    )
    returned = (
        lax.all_to_all(home_query, "seq", split_axis=0, concat_axis=3, tiled=True),
        lax.all_to_all(home_key, "seq", split_axis=0, concat_axis=3, tiled=True),
        lax.all_to_all(home_value, "seq", split_axis=0, concat_axis=3, tiled=True),
    )
    grad_query, grad_key, grad_value = [part.reshape(tok_dev, -1) for part in returned]
    return (grad_query, grad_key, grad_value)


def solution(mesh):
    placed = (
        P(("seq", "rep"), None),
        P(("seq", "rep"), None),
        P(("seq", "rep"), None),
        P(("seq", "rep"), None),
        P(("seq", "rep"), None),
        P(),
    )
    return jax.shard_map(
        shards,
        mesh=mesh,
        in_specs=placed,
        out_specs=(P(("seq", "rep"), None), P(("seq", "rep"), None), P(("seq", "rep"), None)),
        check_vma=False,
    )
```

profile of v0, /device:TPU:13, one launch (start us, length us, event | category | flops | bytes accessed | tf_op | source)
XLA Modules:
  0.0 332.6 jit_solution(13541607327685269739)
XLA Ops:
  0.6 2.1 copy.110
  2.7 6.7 %all-to-all-start = ((bf16[1,1,128,16,128]{2,4,1,0,3:T(8,128)(2,1)}), bf16[1,1,128,16,128]{2,4,1,0,3:T(8,128)(2,1)S(1)}, u32[]{:S(2)}, u32[]{:S(2)}) async-start(bf16[1,1,128,16,128]{2,4,1,0,3:T(8,128)(2,1)} %bitcast.4), calls=%async_computation | async-start | bytes 1048576 | tf_op jit(solution)/shard_map/all_to_all | solution.py:118
  10.4 12.6 %all-to-all-done = bf16[1,1,128,16,128]{2,4,1,0,3:T(8,128)(2,1)S(1)} async-done(((bf16[1,1,128,16,128]{2,4,1,0,3:T(8,128)(2,1)}), bf16[1,1,128,16,128]{2,4,1,0,3:T(8,128)(2,1)S(1)}, u32[]{:S(2)}, u32[]{:S(2)}) %all-to-all-start) | async-done | bytes 524320 | tf_op jit(solution)/shard_map/all_to_all | solution.py:118
  23.0 5.0 %all-to-all-start.2 = ((bf16[1,1,128,16,128]{2,4,1,0,3:T(8,128)(2,1)}), bf16[1,1,128,16,128]{2,4,1,0,3:T(8,128)(2,1)S(1)}, u32[]{:S(2)}, u32[]{:S(2)}) async-start(bf16[1,1,128,16,128]{2,4,1,0,3:T(8,128)(2,1)} %bitcast.13), calls=%async_computation.2 | async-start | bytes 1048576 | tf_op jit(solution)/shard_map/all_to_all | solution.py:125
  29.0 12.6 %all-to-all-done.2 = bf16[1,1,128,16,128]{2,4,1,0,3:T(8,128)(2,1)S(1)} async-done(((bf16[1,1,128,16,128]{2,4,1,0,3:T(8,128)(2,1)}), bf16[1,1,128,16,128]{2,4,1,0,3:T(8,128)(2,1)S(1)}, u32[]{:S(2)}, u32[]{:S(2)}) %all-to-all-start.2) | async-done | bytes 524320 | tf_op jit(solution)/shard_map/all_to_all | solution.py:125
  41.6 5.0 %all-to-all-start.8 = ((bf16[1,1,128,16,128]{2,4,1,0,3:T(8,128)(2,1)}), bf16[1,1,128,16,128]{2,4,1,0,3:T(8,128)(2,1)S(1)}, u32[]{:S(2)}, u32[]{:S(2)}) async-start(bf16[1,1,128,16,128]{2,4,1,0,3:T(8,128)(2,1)} %bitcast.42), calls=%async_computation.8 | async-start | bytes 1048576 | tf_op jit(solution)/shard_map/all_to_all | solution.py:132
  47.6 12.6 %all-to-all-done.8 = bf16[1,1,128,16,128]{2,4,1,0,3:T(8,128)(2,1)S(1)} async-done(((bf16[1,1,128,16,128]{2,4,1,0,3:T(8,128)(2,1)}), bf16[1,1,128,16,128]{2,4,1,0,3:T(8,128)(2,1)S(1)}, u32[]{:S(2)}, u32[]{:S(2)}) %all-to-all-start.8) | async-done | bytes 524320 | tf_op jit(solution)/shard_map/all_to_all | solution.py:132
  60.2 5.0 %all-to-all-start.6 = ((bf16[1,1,128,16,128]{2,4,1,0,3:T(8,128)(2,1)}), bf16[1,1,128,16,128]{2,4,1,0,3:T(8,128)(2,1)}, u32[]{:S(2)}, u32[]{:S(2)}) async-start(bf16[1,1,128,16,128]{2,4,1,0,3:T(8,128)(2,1)} %bitcast.33), calls=%async_computation.6 | async-start | bytes 1048576 | tf_op jit(solution)/shard_map/all_to_all | solution.py:139
  65.4 13.4 %all-to-all-done.6 = bf16[1,1,128,16,128]{2,4,1,0,3:T(8,128)(2,1)} async-done(((bf16[1,1,128,16,128]{2,4,1,0,3:T(8,128)(2,1)}), bf16[1,1,128,16,128]{2,4,1,0,3:T(8,128)(2,1)}, u32[]{:S(2)}, u32[]{:S(2)}) %all-to-all-start.6) | async-done | bytes 524320 | tf_op jit(solution)/shard_map/all_to_all | solution.py:139
  78.9 18.4 %all_to_all.264 = bf16[1,1,128,16,128]{2,4,1,0,3:T(8,128)(2,1)} all-to-all(bf16[1,1,128,16,128]{2,4,1,0,3:T(8,128)(2,1)S(1)} %bitcast.169), channel_id=1, replica_groups=mesh['seq'=16,'rep'=2] {'seq'}, dimensions={3} | all-to-all | bytes 1048576 | tf_op jit(solution)/shard_map/all_to_all | solution.py:148
  97.3 10.1 %all_to_all.265 = bf16[16,1,128,1,128]{2,4,3,1,0:T(8,128)(2,1)S(1)} all-to-all(bf16[16,1,128,1,128]{2,4,3,1,0:T(8,128)(2,1)S(1)} %bitcast.164), channel_id=1, replica_groups=mesh['seq'=16,'rep'=2] {'rep'}, dimensions={0} | all-to-all | bytes 1048576 | tf_op jit(solution)/shard_map/all_to_all | solution.py:117
  107.4 9.2 %all_to_all.266 = bf16[16,1,128,1,128]{2,4,3,1,0:T(8,128)(2,1)S(1)} all-to-all(bf16[16,1,128,1,128]{2,4,3,1,0:T(8,128)(2,1)S(1)} %bitcast.166), channel_id=1, replica_groups=mesh['seq'=16,'rep'=2] {'rep'}, dimensions={0} | all-to-all | bytes 1048576 | tf_op jit(solution)/shard_map/all_to_all | solution.py:124
  116.7 8.3 %all_to_all.267 = bf16[16,1,128,1,128]{2,4,3,1,0:T(8,128)(2,1)S(1)} all-to-all(bf16[16,1,128,1,128]{2,4,3,1,0:T(8,128)(2,1)S(1)} %bitcast.167), channel_id=1, replica_groups=mesh['seq'=16,'rep'=2] {'rep'}, dimensions={0} | all-to-all | bytes 1048576 | tf_op jit(solution)/shard_map/all_to_all | solution.py:131
  125.0 3.5 %all-to-all-start.7 = ((bf16[16,1,128,1,128]{2,4,3,1,0:T(8,128)(2,1)}), bf16[16,1,128,1,128]{2,4,3,1,0:T(8,128)(2,1)S(1)}, u32[]{:S(2)}, u32[]{:S(2)}) async-start(bf16[16,1,128,1,128]{2,4,3,1,0:T(8,128)(2,1)} %bitcast.37), calls=%async_computation.7 | async-start | bytes 1048576 | tf_op jit(solution)/shard_map/all_to_all | solution.py:138
  129.6 4.1 %collective-permute-start = (bf16[1536,128]{1,0:T(8,128)(2,1)}, bf16[1536,128]{1,0:T(8,128)(2,1)}, u32[]{:S(2)}, u32[]{:S(2)}) collective-permute-start(bf16[1536,128]{1,0:T(8,128)(2,1)} %bitcast.20), channel_id=1, source_target_pairs={{0,1},{2,3},{4,5},{6,7},{8,9},{10,11},{12,13},{14,15},{16,17},{18,... | collective-permute-start | bytes 1179656 | tf_op jit(solution)/shard_map/ppermute | solution.py:17
  133.9 3.5 %all-to-all-start.5 = ((bf16[16,1,128,1,128]{2,4,3,1,0:T(8,128)(2,1)}), bf16[16,1,128,1,128]{2,4,3,1,0:T(8,128)(2,1)S(1)}, u32[]{:S(2)}, u32[]{:S(2)}) async-start(bf16[16,1,128,1,128]{2,4,3,1,0:T(8,128)(2,1)} %bitcast.28), calls=%async_computation.5 | async-start | bytes 1048576 | tf_op jit(solution)/shard_map/all_to_all | solution.py:147
  139.9 3.4 %collective-permute-start.1 = (bf16[1536,128]{1,0:T(8,128)(2,1)}, bf16[1536,128]{1,0:T(8,128)(2,1)S(1)}, u32[]{:S(2)}, u32[]{:S(2)}) collective-permute-start(bf16[1536,128]{1,0:T(8,128)(2,1)} %bitcast.49), channel_id=1, source_target_pairs={{0,1},{2,3},{4,5},{6,7},{8,9},{10,11},{12,13},{14,15},{16,17},{18,... | collective-permute-start | bytes 1179656 | tf_op jit(solution)/shard_map/ppermute | solution.py:17
  144.4 2.7 all-to-all-done.5
  149.2 6.2 %collective-permute-done.1 = bf16[1536,128]{1,0:T(8,128)(2,1)S(1)} collective-permute-done((bf16[1536,128]{1,0:T(8,128)(2,1)}, bf16[1536,128]{1,0:T(8,128)(2,1)S(1)}, u32[]{:S(2)}, u32[]{:S(2)}) %collective-permute-start.1) | collective-permute-done | bytes 393248 | tf_op jit(solution)/shard_map/ppermute | solution.py:17
  157.7 1.4 broadcast.112
  159.1 52.7 %while.125 = (s32[]{:T(128)}, f32[2048,128]{1,0:T(8,128)}, f32[3584,128]{1,0:T(8,128)}, f32[3584,128]{1,0:T(8,128)S(1)}, s32[16]{0:T(128)S(1)}, /*index=5*/s32[]...) while((s32[]{:T(128)}, f32[2048,128]{1,0:T(8,128)}, ...), condition=%wide.region_10.11_spmd, body=%wide.region_1.10_spmd.sunk | while | flops 408908320 | bytes 11222327 | solution.py:186
  163.3 4.3 %while.127 = (s32[]{:T(128)}, f32[512,128]{1,0:T(8,128)S(1)}, f32[3584,128]{1,0:T(8,128)}, f32[3584,128]{1,0:T(8,128)S(1)}, s32[]{:T(128)}, /*index=5*/s32[512]{...) while((s32[]{:T(128)}, f32[512,128]{1,0:T(8,128)S(1)}, ...), condition=%wide.region_9.9_spmd.clone, body=%wide.region_8.8_spmd.clone.sunk | while | flops 338363392 | bytes 7223547 | solution.py:99
  165.7 2.0 fusion.62
  171.9 1.6 while.126
  173.5 8.7 %while.127 = (s32[]{:T(128)}, f32[512,128]{1,0:T(8,128)S(1)}, f32[3584,128]{1,0:T(8,128)}, f32[3584,128]{1,0:T(8,128)S(1)}, s32[]{:T(128)}, /*index=5*/s32[512]{...) while((s32[]{:T(128)}, f32[512,128]{1,0:T(8,128)S(1)}, ...), condition=%wide.region_9.9_spmd.clone, body=%wide.region_8.8_spmd.clone.sunk | while | flops 338363392 | bytes 7223547 | solution.py:99
  175.9 2.0 fusion.62
  180.2 2.0 fusion.62
  186.3 1.6 while.126
  187.9 8.7 %while.127 = (s32[]{:T(128)}, f32[512,128]{1,0:T(8,128)S(1)}, f32[3584,128]{1,0:T(8,128)}, f32[3584,128]{1,0:T(8,128)S(1)}, s32[]{:T(128)}, /*index=5*/s32[512]{...) while((s32[]{:T(128)}, f32[512,128]{1,0:T(8,128)S(1)}, ...), condition=%wide.region_9.9_spmd.clone, body=%wide.region_8.8_spmd.clone.sunk | while | flops 338363392 | bytes 7223547 | solution.py:99
  190.3 2.0 fusion.62
  194.7 2.0 fusion.62
  200.8 1.6 while.126
  202.4 8.6 %while.127 = (s32[]{:T(128)}, f32[512,128]{1,0:T(8,128)S(1)}, f32[3584,128]{1,0:T(8,128)}, f32[3584,128]{1,0:T(8,128)S(1)}, s32[]{:T(128)}, /*index=5*/s32[512]{...) while((s32[]{:T(128)}, f32[512,128]{1,0:T(8,128)S(1)}, ...), condition=%wide.region_9.9_spmd.clone, body=%wide.region_8.8_spmd.clone.sunk | while | flops 338363392 | bytes 7223547 | solution.py:99
  204.8 2.0 fusion.62
  209.1 2.0 fusion.62
  214.3 1.3 multiply_convert_fusion.1
  216.4 24.4 %all-to-all-start.10 = ((bf16[8,2,128,1,128]{4,2,0,3,1:T(8,128)(2,1)}), bf16[8,2,128,1,128]{4,2,0,3,1:T(8,128)(2,1)S(1)}, u32[]{:S(2)}, u32[]{:S(2)}) async-start(bf16[8,2,128,1,128]{4,2,0,3,1:T(8,128)(2,1)} %copy.137), calls=%async_computation.10 | async-start | bytes 1048576 | tf_op jit(solution)/shard_map/all_to_all | solution.py:201
  242.2 1.3 collective-permute-done.2
  243.5 1.4 multiply_convert_fusion
  245.8 4.4 %all-to-all-done.10 = bf16[8,2,128,1,128]{4,2,0,3,1:T(8,128)(2,1)S(1)} async-done(((bf16[8,2,128,1,128]{4,2,0,3,1:T(8,128)(2,1)}), bf16[8,2,128,1,128]{4,2,0,3,1:T(8,128)(2,1)S(1)}, u32[]{:S(2)}, u32[]{:S(2)}) %all-to-all-start.10) | async-done | bytes 524320 | tf_op jit(solution)/shard_map/all_to_all | solution.py:201
  250.2 3.5 %all-to-all-start.12 = ((bf16[8,2,128,1,128]{4,2,0,3,1:T(8,128)(2,1)}), bf16[8,2,128,1,128]{4,2,0,3,1:T(8,128)(2,1)S(1)}, u32[]{:S(2)}, u32[]{:S(2)}) async-start(bf16[8,2,128,1,128]{4,2,0,3,1:T(8,128)(2,1)} %copy.140), calls=%async_computation.12 | async-start | bytes 1048576 | tf_op jit(solution)/shard_map/all_to_all | solution.py:204
  253.7 5.0 %collective-permute-done.3 = bf16[1536,128]{1,0:T(8,128)(2,1)} collective-permute-done((bf16[1536,128]{1,0:T(8,128)(2,1)S(1)}, bf16[1536,128]{1,0:T(8,128)(2,1)}, u32[]{:S(2)}, u32[]{:S(2)}) %collective-permute-start.3) | collective-permute-done | bytes 393248 | tf_op jit(solution)/shard_map/ppermute | solution.py:17
  259.9 4.4 %all-to-all-done.12 = bf16[8,2,128,1,128]{4,2,0,3,1:T(8,128)(2,1)S(1)} async-done(((bf16[8,2,128,1,128]{4,2,0,3,1:T(8,128)(2,1)}), bf16[8,2,128,1,128]{4,2,0,3,1:T(8,128)(2,1)S(1)}, u32[]{:S(2)}, u32[]{:S(2)}) %all-to-all-start.12) | async-done | bytes 524320 | tf_op jit(solution)/shard_map/all_to_all | solution.py:204
  264.2 9.0 %all_to_all.268 = bf16[8,2,128,1,128]{4,2,0,3,1:T(8,128)(2,1)} all-to-all(bf16[8,2,128,1,128]{4,2,0,3,1:T(8,128)(2,1)S(1)} %copy.143), channel_id=1, replica_groups=mesh['seq'=16,'rep'=2] {'rep'}, dimensions={1} | all-to-all | bytes 1048576 | tf_op jit(solution)/shard_map/all_to_all | solution.py:207
  273.2 21.2 %all_to_all.269 = bf16[16,1,128,1,128]{4,2,3,1,0:T(8,128)(2,1)S(1)} all-to-all(bf16[16,1,128,1,128]{4,2,3,1,0:T(8,128)(2,1)S(1)} %bitcast.165), channel_id=1, replica_groups=mesh['seq'=16,'rep'=2] {'seq'}, dimensions={0} | all-to-all | bytes 1048576 | tf_op jit(solution)/shard_map/all_to_all | solution.py:210
  294.4 18.4 %all_to_all.270 = bf16[16,1,128,1,128]{4,2,3,1,0:T(8,128)(2,1)S(1)} all-to-all(bf16[16,1,128,1,128]{4,2,3,1,0:T(8,128)(2,1)S(1)} %bitcast.168), channel_id=1, replica_groups=mesh['seq'=16,'rep'=2] {'seq'}, dimensions={0} | all-to-all | bytes 1048576 | tf_op jit(solution)/shard_map/all_to_all | solution.py:211
  312.8 5.0 %all-to-all-start.15 = ((bf16[16,1,128,1,128]{4,2,3,1,0:T(8,128)(2,1)}), bf16[16,1,128,1,128]{4,2,3,1,0:T(8,128)(2,1)S(1)}, u32[]{:S(2)}, u32[]{:S(2)}) async-start(bf16[16,1,128,1,128]{4,2,3,1,0:T(8,128)(2,1)} %bitcast.72), calls=%async_computation.15 | async-start | bytes 1048576 | tf_op jit(solution)/shard_map/all_to_all | solution.py:212
  320.4 11.0 %all-to-all-done.15 = bf16[16,1,128,1,128]{4,2,3,1,0:T(8,128)(2,1)S(1)} async-done(((bf16[16,1,128,1,128]{4,2,3,1,0:T(8,128)(2,1)}), bf16[16,1,128,1,128]{4,2,3,1,0:T(8,128)(2,1)S(1)}, u32[]{:S(2)}, u32[]{:S(2)}) %all-to-all-start.15) | async-done | bytes 524320 | tf_op jit(solution)/shard_map/all_to_all | solution.py:212
  (173 shorter events, 59.3 us)
Async XLA Ops:
  0.6 8.8 %copy-start = (bf16[128,2048]{1,0:T(8,128)(2,1)S(1)}, bf16[128,2048]{1,0:T(8,128)(2,1)}, u32[]{:S(2)}) copy-start(bf16[128,2048]{1,0:T(8,128)(2,1)} %param.13) | copy-start | bytes 1572868
  2.7 25.3 %copy-start.1 = (bf16[128,2048]{1,0:T(8,128)(2,1)S(1)}, bf16[128,2048]{1,0:T(8,128)(2,1)}, u32[]{:S(2)}) copy-start(bf16[128,2048]{1,0:T(8,128)(2,1)} %param.14) | copy-start | bytes 1572868
  2.7 20.3 %all-to-all-start = ((bf16[1,1,128,16,128]{2,4,1,0,3:T(8,128)(2,1)}), bf16[1,1,128,16,128]{2,4,1,0,3:T(8,128)(2,1)S(1)}, u32[]{:S(2)}, u32[]{:S(2)}) async-start(bf16[1,1,128,16,128]{2,4,1,0,3:T(8,128)(2,1)} %bitcast.4), calls=%async_computation | async-start | bytes 1048576 | tf_op jit(solution)/shard_map/all_to_all | solution.py:118
  10.4 36.1 %copy-start.2 = (bf16[128,2048]{1,0:T(8,128)(2,1)S(1)}, bf16[128,2048]{1,0:T(8,128)(2,1)}, u32[]{:S(2)}) copy-start(bf16[128,2048]{1,0:T(8,128)(2,1)} %param.15) | copy-start | bytes 1572868
  23.0 18.6 %all-to-all-start.2 = ((bf16[1,1,128,16,128]{2,4,1,0,3:T(8,128)(2,1)}), bf16[1,1,128,16,128]{2,4,1,0,3:T(8,128)(2,1)S(1)}, u32[]{:S(2)}, u32[]{:S(2)}) async-start(bf16[1,1,128,16,128]{2,4,1,0,3:T(8,128)(2,1)} %bitcast.13), calls=%async_computation.2 | async-start | bytes 1048576 | tf_op jit(solution)/shard_map/all_to_all | solution.py:125
  29.0 36.1 %copy-start.3 = (bf16[128,2048]{1,0:T(8,128)(2,1)S(1)}, bf16[128,2048]{1,0:T(8,128)(2,1)}, u32[]{:S(2)}) copy-start(bf16[128,2048]{1,0:T(8,128)(2,1)} %param.16) | copy-start | bytes 1572868
  41.6 18.6 %all-to-all-start.8 = ((bf16[1,1,128,16,128]{2,4,1,0,3:T(8,128)(2,1)}), bf16[1,1,128,16,128]{2,4,1,0,3:T(8,128)(2,1)S(1)}, u32[]{:S(2)}, u32[]{:S(2)}) async-start(bf16[1,1,128,16,128]{2,4,1,0,3:T(8,128)(2,1)} %bitcast.42), calls=%async_computation.8 | async-start | bytes 1048576 | tf_op jit(solution)/shard_map/all_to_all | solution.py:132
  60.2 18.7 %all-to-all-start.6 = ((bf16[1,1,128,16,128]{2,4,1,0,3:T(8,128)(2,1)}), bf16[1,1,128,16,128]{2,4,1,0,3:T(8,128)(2,1)}, u32[]{:S(2)}, u32[]{:S(2)}) async-start(bf16[1,1,128,16,128]{2,4,1,0,3:T(8,128)(2,1)} %bitcast.33), calls=%async_computation.6 | async-start | bytes 1048576 | tf_op jit(solution)/shard_map/all_to_all | solution.py:139
  125.0 8.9 %all-to-all-start.7 = ((bf16[16,1,128,1,128]{2,4,3,1,0:T(8,128)(2,1)}), bf16[16,1,128,1,128]{2,4,3,1,0:T(8,128)(2,1)S(1)}, u32[]{:S(2)}, u32[]{:S(2)}) async-start(bf16[16,1,128,1,128]{2,4,3,1,0:T(8,128)(2,1)} %bitcast.37), calls=%async_computation.7 | async-start | bytes 1048576 | tf_op jit(solution)/shard_map/all_to_all | solution.py:138
  128.4 8.9 %copy-start.4 = (s32[16]{0:T(128)S(1)}, s32[16]{0:T(128)}, u32[]{:S(2)}) copy-start(s32[16]{0:T(128)} %param.17) | copy-start | bytes 196
  129.6 18.6 %collective-permute-start = (bf16[1536,128]{1,0:T(8,128)(2,1)}, bf16[1536,128]{1,0:T(8,128)(2,1)}, u32[]{:S(2)}, u32[]{:S(2)}) collective-permute-start(bf16[1536,128]{1,0:T(8,128)(2,1)} %bitcast.20), channel_id=1, source_target_pairs={{0,1},{2,3},{4,5},{6,7},{8,9},{10,11},{12,13},{14,15},{16,17},{18,... | collective-permute-start | bytes 1179656 | tf_op jit(solution)/shard_map/ppermute | solution.py:17
  133.9 13.2 %all-to-all-start.5 = ((bf16[16,1,128,1,128]{2,4,3,1,0:T(8,128)(2,1)}), bf16[16,1,128,1,128]{2,4,3,1,0:T(8,128)(2,1)S(1)}, u32[]{:S(2)}, u32[]{:S(2)}) async-start(bf16[16,1,128,1,128]{2,4,3,1,0:T(8,128)(2,1)} %bitcast.28), calls=%async_computation.5 | async-start | bytes 1048576 | tf_op jit(solution)/shard_map/all_to_all | solution.py:147
  139.9 15.6 %collective-permute-start.1 = (bf16[1536,128]{1,0:T(8,128)(2,1)}, bf16[1536,128]{1,0:T(8,128)(2,1)S(1)}, u32[]{:S(2)}, u32[]{:S(2)}) collective-permute-start(bf16[1536,128]{1,0:T(8,128)(2,1)} %bitcast.49), channel_id=1, source_target_pairs={{0,1},{2,3},{4,5},{6,7},{8,9},{10,11},{12,13},{14,15},{16,17},{18,... | collective-permute-start | bytes 1179656 | tf_op jit(solution)/shard_map/ppermute | solution.py:17
  213.0 30.6 %collective-permute-start.2 = (bf16[1536,128]{1,0:T(8,128)(2,1)S(1)}, bf16[1536,128]{1,0:T(8,128)(2,1)}, u32[]{:S(2)}, u32[]{:S(2)}) collective-permute-start(bf16[1536,128]{1,0:T(8,128)(2,1)S(1)} %slice.56), channel_id=1, source_target_pairs={{1,0},{3,2},{5,4},{7,6},{9,8},{11,10},{13,12},{15,14},{17,16},{19,... | collective-permute-start | bytes 1179656 | tf_op jit(solution)/shard_map/ppermute | solution.py:17
  216.4 33.8 %all-to-all-start.10 = ((bf16[8,2,128,1,128]{4,2,0,3,1:T(8,128)(2,1)}), bf16[8,2,128,1,128]{4,2,0,3,1:T(8,128)(2,1)S(1)}, u32[]{:S(2)}, u32[]{:S(2)}) async-start(bf16[8,2,128,1,128]{4,2,0,3,1:T(8,128)(2,1)} %copy.137), calls=%async_computation.10 | async-start | bytes 1048576 | tf_op jit(solution)/shard_map/all_to_all | solution.py:201
  240.9 17.8 %collective-permute-start.3 = (bf16[1536,128]{1,0:T(8,128)(2,1)S(1)}, bf16[1536,128]{1,0:T(8,128)(2,1)}, u32[]{:S(2)}, u32[]{:S(2)}) collective-permute-start(bf16[1536,128]{1,0:T(8,128)(2,1)S(1)} %slice.55), channel_id=1, source_target_pairs={{1,0},{3,2},{5,4},{7,6},{9,8},{11,10},{13,12},{15,14},{17,16},{19,... | collective-permute-start | bytes 1179656 | tf_op jit(solution)/shard_map/ppermute | solution.py:17
  250.2 14.0 %all-to-all-start.12 = ((bf16[8,2,128,1,128]{4,2,0,3,1:T(8,128)(2,1)}), bf16[8,2,128,1,128]{4,2,0,3,1:T(8,128)(2,1)S(1)}, u32[]{:S(2)}, u32[]{:S(2)}) async-start(bf16[8,2,128,1,128]{4,2,0,3,1:T(8,128)(2,1)} %copy.140), calls=%async_computation.12 | async-start | bytes 1048576 | tf_op jit(solution)/shard_map/all_to_all | solution.py:204
  312.8 18.6 %all-to-all-start.15 = ((bf16[16,1,128,1,128]{4,2,3,1,0:T(8,128)(2,1)}), bf16[16,1,128,1,128]{4,2,3,1,0:T(8,128)(2,1)S(1)}, u32[]{:S(2)}, u32[]{:S(2)}) async-start(bf16[16,1,128,1,128]{4,2,3,1,0:T(8,128)(2,1)} %bitcast.72), calls=%async_computation.15 | async-start | bytes 1048576 | tf_op jit(solution)/shard_map/all_to_all | solution.py:212
where the time goes:
time: 331 us; the launch traced here: 333 us
  blocking collectives  94.6 us (29%)
  waiting for transfers between devices  86.4 us (26%)
  starting transfers between devices  71.5 us (22%)
  matrix products  32.7 us (10%)
  local copies, waits for them, and re-layouts  29.7 us (9%)
  other arithmetic  13.3 us (4%)
  loops' own time  3.55 us (1%)
    all_to_all x1, starting transfers between devices, shards(): lax.all_to_all(to_tokens(dq_own, softmax_scale), 'rep', split_axis=1, con...  24.4 us
    all_to_all x1, blocking collectives, shards(): lax.all_to_all(home_query, 'seq', split_axis=0, concat_axis=3, tiled=True)  21.2 us
    all_to_all x1, blocking collectives, shards(): lax.all_to_all(split_heads(grad_output), 'seq', split_axis=3, concat_axis...  18.4 us
    all_to_all x1, blocking collectives, shards(): lax.all_to_all(home_key, 'seq', split_axis=0, concat_axis=3, tiled=True)  18.4 us
    dot_general x7, matrix products, grad_step(): lax.dot_general(dscore, query_tile, (((0,), (0,)), ((), ())), preferred_e...  13.7 us
    all_to_all x1, waiting for transfers between devices, shards(): lax.all_to_all(split_heads(saved_output), 'seq', split_axis=3, concat_axi...  13.4 us
    ppermute x4, waiting for transfers between devices, shifted(): return lax.ppermute(array, axis, pairs)  12.6 us
    all_to_all x1, waiting for transfers between devices, shards(): lax.all_to_all(split_heads(value_rows), 'seq', split_axis=3, concat_axis=...  12.6 us
  transfers between devices with their start and end apart: 13, of which 12 were waited for; matrix products, arithmetic and copies ran while one was open for 6% of the time, Pallas kernels for 0%

commit v1 on v0

v1 whole, which is shorter than its diff:
```python
import functools

import jax
import jax.numpy as jnp
from jax import lax
from jax.experimental import pallas as pl
from jax.experimental.pallas import tpu as pltpu
from jax.sharding import PartitionSpec as P

HEAD_DIM = 128
TILE = 512
BAND = 512
CHUNK = 256
PAIR = 2
NEG_FILL = -1e30
SCALE = HEAD_DIM ** (-0.5)
MESH = pl.DeviceIdType.MESH
NT = (((1,), (1,)), ((), ()))
NN = (((1,), (0,)), ((), ()))
TN = (((0,), (0,)), ((), ()))


def greet(groups, helpers, me, rep):
    barrier = pltpu.get_barrier_semaphore()

    def to_group(step, carry):
        pl.semaphore_signal(
            barrier, inc=1, device_id=(lax.rem(me + step, groups), rep), device_id_type=MESH
        )
        return carry

    lax.fori_loop(1, groups, to_group, 0)
    for step in range(1, helpers):
        pl.semaphore_signal(
            barrier, inc=1, device_id=(me, lax.rem(rep + step, helpers)), device_id_type=MESH
        )
    pl.semaphore_wait(barrier, groups - 1 + helpers - 1)


def spread_kernel(
    groups,
    helpers,
    q_ref,
    k_ref,
    v_ref,
    o_ref,
    do_ref,
    qr,
    kr,
    vr,
    dor,
    dlr,
    delta,
    send_sem,
    recv_sem,
    fsend_sem,
    frecv_sem,
    own_sem,
):
    me = lax.axis_index("seq")
    rep = lax.axis_index("rep")
    greet(groups, helpers, me, rep)

    def columns(ref, head):
        return ref.at[:, pl.ds(pl.multiple_of(head * HEAD_DIM, HEAD_DIM), HEAD_DIM)]

    pairs = (
        (k_ref, lambda s: kr.at[s, rep]),
        (v_ref, lambda s: vr.at[s, rep]),
        (q_ref, lambda s: qr.at[s]),
        (do_ref, lambda s: dor.at[s]),
    )

    def outgoing(which, step):
        to = lax.rem(me + step, groups)
        src, dst = pairs[which]
        return pltpu.make_async_remote_copy(
            src_ref=columns(src, to),
            dst_ref=dst(me),
            send_sem=send_sem.at[which, step],
            recv_sem=recv_sem.at[which, step],
            device_id=(to, rep),
            device_id_type=MESH,
        )

    def arriving(which, step):
        source = lax.rem(me + groups - step, groups)
        src, dst = pairs[which]
        return pltpu.make_async_remote_copy(
            src_ref=columns(src, source),
            dst_ref=dst(source),
            send_sem=send_sem.at[which, step],
            recv_sem=recv_sem.at[which, step],
            device_id=(source, rep),
            device_id_type=MESH,
        )

    def own(which):
        src, dst = pairs[which]
        return pltpu.make_async_copy(columns(src, me), dst(me), own_sem.at[which])

    def forward(which, source, hop):
        dst = pairs[which][1]
        return pltpu.make_async_remote_copy(
            src_ref=dst(source),
            dst_ref=dst(source),
            send_sem=fsend_sem.at[which, hop - 1, source],
            recv_sem=frecv_sem.at[which, hop - 1, source],
            device_id=(me, lax.rem(rep + hop, helpers)),
            device_id_type=MESH,
        )

    def forwarded(which, source, hop):
        other = lax.rem(rep + helpers - hop, helpers)
        ref = (kr, vr)[which].at[source, other]
        return pltpu.make_async_remote_copy(
            src_ref=ref,
            dst_ref=ref,
            send_sem=fsend_sem.at[which, hop - 1, source],
            recv_sem=frecv_sem.at[which, hop - 1, source],
            device_id=(me, other),
            device_id_type=MESH,
        )

    for which in range(4):
        own(which).start()

        def send(step, carry, which=which):
            outgoing(which, step).start()
            return carry

        lax.fori_loop(1, groups, send, 0)

    def head_delta(head, carry):
        cols = pl.ds(pl.multiple_of(head * HEAD_DIM, HEAD_DIM), HEAD_DIM)
        prod = do_ref[:, cols].astype(jnp.float32) * o_ref[:, cols].astype(jnp.float32)
        row = jnp.sum(prod.T, axis=0, keepdims=True)
        delta[head] = jnp.broadcast_to(row, delta.shape[1:])
        return carry

    lax.fori_loop(0, groups, head_delta, 0)

    def delta_out(step):
        to = lax.rem(me + step, groups)
        return pltpu.make_async_remote_copy(
            src_ref=delta.at[to],
            dst_ref=dlr.at[me],
            send_sem=send_sem.at[4, step],
            recv_sem=recv_sem.at[4, step],
            device_id=(to, rep),
            device_id_type=MESH,
        )

    def delta_in(step):
        source = lax.rem(me + groups - step, groups)
        return pltpu.make_async_remote_copy(
            src_ref=delta.at[source],
            dst_ref=dlr.at[source],
            send_sem=send_sem.at[4, step],
            recv_sem=recv_sem.at[4, step],
            device_id=(source, rep),
            device_id_type=MESH,
        )

    own_delta = pltpu.make_async_copy(delta.at[me], dlr.at[me], own_sem.at[4])
    own_delta.start()

    def send_delta(step, carry):
        delta_out(step).start()
        return carry

    lax.fori_loop(1, groups, send_delta, 0)

    for which in range(2):
        own(which).wait()
        for hop in range(1, helpers):
            forward(which, me, hop).start()

        def relay(step, carry, which=which):
            arriving(which, step).wait_recv()
            for hop in range(1, helpers):
                forward(which, lax.rem(me + groups - step, groups), hop).start()
            return carry

        lax.fori_loop(1, groups, relay, 0)
    for which in range(2, 4):
        own(which).wait()

        def take(step, carry, which=which):
            arriving(which, step).wait_recv()
            return carry

        lax.fori_loop(1, groups, take, 0)

    own_delta.wait()

    def finish(step, carry):
        delta_in(step).wait_recv()
        delta_out(step).wait_send()
        for which in range(4):
            outgoing(which, step).wait_send()
        return carry

    lax.fori_loop(1, groups, finish, 0)

    def finish_forward(source, carry):
        for which in range(2):
            for hop in range(1, helpers):
                forwarded(which, source, hop).wait_recv()
                forward(which, source, hop).wait_send()
        return carry

    lax.fori_loop(0, groups, finish_forward, 0)


def attend_kernel(
    groups,
    helpers,
    tok,
    docs_ref,
    q_ref,
    k_ref,
    v_ref,
    do_ref,
    dl_ref,
    dq_ref,
    dk_ref,
    dv_ref,
    s_ref,
    dk_acc,
    dv_acc,
):
    rep = lax.axis_index("rep")
    total = groups * helpers * tok
    width = PAIR * tok
    docs = docs_ref.shape[0]

    def clear(c, carry):
        rows = pl.ds(pl.multiple_of(c * CHUNK, CHUNK), CHUNK)
        dk_acc[rows, :] = jnp.zeros((CHUNK, HEAD_DIM), jnp.float32)
        dv_acc[rows, :] = jnp.zeros((CHUNK, HEAD_DIM), jnp.float32)
        return carry

    lax.fori_loop(0, total // CHUNK, clear, 0)

    def tile(t, carry):
        lane = lax.broadcasted_iota(jnp.int32, (1, width), 1)
        row = ((t * PAIR + lane // tok) * helpers + rep) * tok + lane % tok
        first = (t * PAIR * helpers + rep) * tok
        last = ((t * PAIR + PAIR - 1) * helpers + rep) * tok + tok - 1

        def per_doc(d, state):
            end, start, starts = state
            end = end + docs_ref[d]
            return (
                end,
                jnp.where(end <= first, end, start),
                jnp.where(end <= row, end, starts),
            )

        unused, start, starts = lax.fori_loop(
            0, docs, per_doc, (jnp.int32(0), jnp.int32(0), jnp.zeros((1, width), jnp.int32))
        )
        low = jnp.minimum(starts, row - (BAND - 1))
        lo = jnp.maximum(jnp.minimum(start, first - (BAND - 1)), 0) // CHUNK
        hi = last // CHUNK + 1
        mine = pl.ds(pl.multiple_of(t * width, width), width)
        queries = q_ref[mine, :]
        douts = do_ref[mine, :]

        def stat(c, state):
            top, norm = state
            keys = k_ref[pl.ds(pl.multiple_of(c * CHUNK, CHUNK), CHUNK), :]
            scores = lax.dot_general(keys, queries, NT, preferred_element_type=jnp.float32) * SCALE
            kid = lax.broadcasted_iota(jnp.int32, (CHUNK, width), 0)
            base = c * CHUNK
            allowed = (kid <= row - base) & (kid >= low - base)
            scores = jnp.where(allowed, scores, NEG_FILL)
            s_ref[pl.ds(pl.multiple_of((c - lo) * CHUNK, CHUNK), CHUNK), :] = scores
            new_top = jnp.maximum(top, jnp.max(scores, axis=0, keepdims=True))
            fresh = jnp.sum(jnp.exp(scores - new_top), axis=0, keepdims=True)
            return new_top, norm * jnp.exp(top - new_top) + fresh

        top, norm = lax.fori_loop(
            lo,
            hi,
            stat,
            (jnp.full((1, width), NEG_FILL, jnp.float32), jnp.zeros((1, width), jnp.float32)),
        )
        log_norm = top + jnp.log(norm)
        delta = jnp.concatenate([dl_ref[t * PAIR + i, 0:1, :] for i in range(PAIR)], axis=1)

        def grad(c, dq):
            rows = pl.ds(pl.multiple_of(c * CHUNK, CHUNK), CHUNK)
            scores = s_ref[pl.ds(pl.multiple_of((c - lo) * CHUNK, CHUNK), CHUNK), :]
            weights = jnp.exp(scores - log_norm)
            grad_weights = lax.dot_general(
                v_ref[rows, :], douts, NT, preferred_element_type=jnp.float32
            )
            dscore = (weights * (grad_weights - delta)).astype(jnp.bfloat16)
            dv_acc[rows, :] += lax.dot_general(
                weights.astype(jnp.bfloat16), douts, NN, preferred_element_type=jnp.float32
            )
            dk_acc[rows, :] += lax.dot_general(
                dscore, queries, NN, preferred_element_type=jnp.float32
            )
            return dq + lax.dot_general(
                k_ref[rows, :], dscore, TN, preferred_element_type=jnp.float32
            )

        dq = lax.fori_loop(lo, hi, grad, jnp.zeros((HEAD_DIM, width), jnp.float32))
        dq_ref[mine, :] = (dq.T * SCALE).astype(jnp.bfloat16)
        return carry

    lax.fori_loop(0, groups // PAIR, tile, 0)

    def settle(c, carry):
        rows = pl.ds(pl.multiple_of(c * CHUNK, CHUNK), CHUNK)
        dk_ref[rows, :] = (dk_acc[rows, :] * SCALE).astype(jnp.bfloat16)
        dv_ref[rows, :] = dv_acc[rows, :].astype(jnp.bfloat16)
        return carry

    lax.fori_loop(0, total // CHUNK, settle, 0)


def gather_kernel(
    groups,
    helpers,
    dq_ref,
    dk_ref,
    dv_ref,
    gq,
    gk,
    gv,
    part,
    summed,
    send_sem,
    recv_sem,
    psend_sem,
    precv_sem,
    own_sem,
):
    me = lax.axis_index("seq")
    rep = lax.axis_index("rep")
    greet(groups, helpers, me, rep)
    partials = (dk_ref, dv_ref)
    results = (gk, gv, gq)

    def columns(ref, head):
        return ref.at[:, pl.ds(pl.multiple_of(head * HEAD_DIM, HEAD_DIM), HEAD_DIM)]

    def share(which, step, hop):
        to_rep = lax.rem(rep + hop, helpers)
        block = lax.rem(me + step, groups)
        return pltpu.make_async_remote_copy(
            src_ref=partials[which].at[block, to_rep],
            dst_ref=part.at[which, hop - 1, block],
            send_sem=psend_sem.at[which, hop - 1, step],
            recv_sem=precv_sem.at[which, hop - 1, step],
            device_id=(me, to_rep),
            device_id_type=MESH,
        )

    def source_of(which, block):
        return dq_ref.at[block] if which == 2 else summed.at[which, block]

    def home(which, step):
        to = lax.rem(me + step, groups)
        return pltpu.make_async_remote_copy(
            src_ref=source_of(which, to),
            dst_ref=columns(results[which], me),
            send_sem=send_sem.at[which, step],
            recv_sem=recv_sem.at[which, step],
            device_id=(to, rep),
            device_id_type=MESH,
        )

    def came(which, step):
        source = lax.rem(me + groups - step, groups)
        return pltpu.make_async_remote_copy(
            src_ref=source_of(which, source),
            dst_ref=columns(results[which], source),
            send_sem=send_sem.at[which, step],
            recv_sem=recv_sem.at[which, step],
            device_id=(source, rep),
            device_id_type=MESH,
        )

    def own(which):
        return pltpu.make_async_copy(
            source_of(which, me), columns(results[which], me), own_sem.at[which]
        )

    for which in range(2):

        def start_share(step, carry, which=which):
            for hop in range(1, helpers):
                share(which, step, hop).start()
            return carry

        lax.fori_loop(0, groups, start_share, 0)

    def start_query(step, carry):
        home(2, step).start()
        return carry

    lax.fori_loop(1, groups, start_query, 0)
    own(2).start()

    def add(which, step):
        block = lax.rem(me + step, groups)
        value = partials[which][block, rep].astype(jnp.float32)
        for hop in range(1, helpers):
            share(which, step, hop).wait_recv()
            value = value + part[which, hop - 1, block].astype(jnp.float32)
        summed[which, block] = value.astype(jnp.bfloat16)

    for which in range(2):

        def add_send(step, carry, which=which):
            add(which, step)
            home(which, step).start()
            return carry

        lax.fori_loop(1, groups, add_send, 0)
        add(which, 0)
        own(which).start()

    for which in range(3):
        own(which).wait()

    def finish(step, carry):
        for which in range(3):
            home(which, step).wait_send()
            came(which, step).wait_recv()
        return carry

    lax.fori_loop(1, groups, finish, 0)

    def finish_share(step, carry):
        for which in range(2):
            for hop in range(1, helpers):
                share(which, step, hop).wait_send()
        return carry

    lax.fori_loop(0, groups, finish_share, 0)


def shards(queries, key_rows, value_rows, saved_output, grad_output, doc_lengths):
    groups = lax.axis_size("seq")
    helpers = lax.axis_size("rep")
    tok = queries.shape[0]
    total = tok * groups * helpers
    longest = tok * groups - TILE
    low = jnp.bfloat16
    dma = pltpu.SemaphoreType.DMA
    anywhere = pl.BlockSpec(memory_space=pl.ANY)
    in_vmem = pl.BlockSpec(memory_space=pltpu.VMEM)
    block = (tok, HEAD_DIM)
    q, k, v, do, delta = pl.pallas_call(
        functools.partial(spread_kernel, groups, helpers),
        out_shape=(
            jax.ShapeDtypeStruct((groups, *block), low),
            jax.ShapeDtypeStruct((groups, helpers, *block), low),
            jax.ShapeDtypeStruct((groups, helpers, *block), low),
            jax.ShapeDtypeStruct((groups, *block), low),
            jax.ShapeDtypeStruct((groups, 8, tok), jnp.float32),
        ),
        in_specs=[anywhere, anywhere, anywhere, in_vmem, in_vmem],
        out_specs=[anywhere] * 5,
        scratch_shapes=[
            pltpu.VMEM((groups, 8, tok), jnp.float32),
            dma((5, groups)),
            dma((5, groups)),
            dma((2, helpers - 1, groups)),
            dma((2, helpers - 1, groups)),
            dma((5,)),
        ],
        compiler_params=pltpu.CompilerParams(
            collective_id=0, has_side_effects=True, vmem_limit_bytes=16 << 20
        ),
        name="spread",
    )(queries, key_rows, value_rows, saved_output, grad_output)

    reach = (PAIR - 1) * helpers * tok + tok + max(longest, BAND)
    window = min(total, (reach // CHUNK + 2) * CHUNK)
    dq, dk, dv = pl.pallas_call(
        functools.partial(attend_kernel, groups, helpers, tok),
        out_shape=(
            jax.ShapeDtypeStruct((groups * tok, HEAD_DIM), low),
            jax.ShapeDtypeStruct((total, HEAD_DIM), low),
            jax.ShapeDtypeStruct((total, HEAD_DIM), low),
        ),
        in_specs=[pl.BlockSpec(memory_space=pltpu.SMEM)] + [in_vmem] * 5,
        out_specs=[in_vmem] * 3,
        scratch_shapes=[
            pltpu.VMEM((window, PAIR * tok), jnp.float32),
            pltpu.VMEM((total, HEAD_DIM), jnp.float32),
            pltpu.VMEM((total, HEAD_DIM), jnp.float32),
        ],
        compiler_params=pltpu.CompilerParams(vmem_limit_bytes=56 << 20),
        name="attend",
    )(
        doc_lengths,
        q.reshape(-1, HEAD_DIM),
        k.reshape(-1, HEAD_DIM),
        v.reshape(-1, HEAD_DIM),
        do.reshape(-1, HEAD_DIM),
        delta,
    )

    return pl.pallas_call(
        functools.partial(gather_kernel, groups, helpers),
        out_shape=(jax.ShapeDtypeStruct(queries.shape, low),) * 3,
        in_specs=[anywhere, in_vmem, in_vmem],
        out_specs=[anywhere] * 3,
        scratch_shapes=[
            pltpu.VMEM((2, helpers - 1, groups, *block), low),
            pltpu.VMEM((2, groups, *block), low),
            dma((3, groups)),
            dma((3, groups)),
            dma((2, helpers - 1, groups)),
            dma((2, helpers - 1, groups)),
            dma((3,)),
        ],
        compiler_params=pltpu.CompilerParams(
            collective_id=1, has_side_effects=True, vmem_limit_bytes=48 << 20
        ),
        name="gather",
    )(
        dq.reshape(groups, *block),
        dk.reshape(groups, helpers, *block),
        dv.reshape(groups, helpers, *block),
    )


def solution(mesh):
    tokens = P(("seq", "rep"), None)
    return jax.shard_map(
        shards,
        mesh=mesh,
        in_specs=(tokens,) * 5 + (P(),),
        out_specs=(tokens,) * 3,
        check_vma=False,
    )
```

time: 331 us -> 141 us (0.43)
  Pallas kernels: 0 us -> 124 us
  blocking collectives: 94.6 us -> 0 us
  waiting for transfers between devices: 86.4 us -> 0 us
  starting transfers between devices: 71.5 us -> 0 us
  matrix products: 32.7 us -> 0 us
  local copies, waits for them, and re-layouts: 29.7 us -> 15.2 us
  other arithmetic: 13.3 us -> 0 us
  loops' own time: 3.55 us -> 0 us
    pallas_call x0 -> x3, Pallas kernels: none -> 124 us  [the longest x1 54 us: shards(): pl.pallas_call(functools.partial(spread_kernel, groups, helpers), out_sha...]
    all_to_all x7 -> x0, blocking collectives: 94.6 us -> none  [the longest x1 21.2 us: shards(): lax.all_to_all(home_query, 'seq', split_axis=0, concat_axis=3, tiled=True)]
    all_to_all x9 -> x0, waiting for transfers between devices: 73.8 us -> none  [the longest x1 13.4 us: shards(): lax.all_to_all(split_heads(saved_output), 'seq', split_axis=3, concat_axi...]
    all_to_all x9 -> x0, starting transfers between devices: 61.5 us -> none  [the longest x1 24.4 us: shards(): lax.all_to_all(to_tokens(dq_own, softmax_scale), 'rep', split_axis=1, con...]
    dot_general x42 -> x0, matrix products: 32.7 us -> none  [the longest x7 13.7 us: grad_step(): lax.dot_general(dscore, query_tile, (((0,), (0,)), ((), ())), preferred_e...]
    ppermute x4 -> x0, waiting for transfers between devices: 12.6 us -> none  [shifted(): return lax.ppermute(array, axis, pairs)]
    ppermute x4 -> x0, starting transfers between devices: 10 us -> none  [shifted(): return lax.ppermute(array, axis, pairs)]
    reduce_sum x15 -> x0, other arithmetic: 7.03 us -> none  [the longest x4 4.45 us: tile_grads(): jnp.sum(dout_tile.astype(jnp.float32) * output_tile.astype(jnp.float32),...]
  transfers between devices with their start and end apart: 13 -> 0, of which waited for: 12 -> 0; matrix products, arithmetic and copies ran while one was open for 6% -> 0% of each run, Pallas kernels for 0% -> 0%
where the time goes in v1:
time: 141 us; the launch traced here: 140 us
  Pallas kernels  124 us (88%)
  local copies, waits for them, and re-layouts  15.2 us (11%)
    pallas_call x1, Pallas kernels, shards(): pl.pallas_call(functools.partial(spread_kernel, groups, helpers), out_sha...  54 us
    pallas_call x1, Pallas kernels, shards(): pl.pallas_call(functools.partial(gather_kernel, groups, helpers), out_sha...  40.1 us
    pallas_call x1, Pallas kernels, shards(): pl.pallas_call(functools.partial(attend_kernel, groups, helpers, tok), ou...  30.3 us
    unnamed x29, local copies, waits for them, and re-layouts  15.2 us

profile of v1, /device:TPU:13, one launch (start us, length us, event | category | flops | bytes accessed | tf_op | source)
XLA Modules:
  0.0 140.3 jit_solution(12396626540968545160)
XLA Ops:
  0.6 0.0 copy-start.4
  0.6 1.0 copy-done.4
  1.7 0.0 copy-start.5
  1.7 1.0 copy-done.5
  2.7 0.0 copy-start.6
  2.7 1.0 copy-done.6
  3.8 0.0 copy-start.7
  3.8 1.0 copy-done.7
  4.8 0.0 copy-start.8
  4.8 1.0 copy-done.8
  5.8 54.0 %spread.1 = (bf16[16,128,128]{2,1,0:T(8,128)(2,1)S(1)}, bf16[16,2,128,128]{3,2,1,0:T(8,128)(2,1)S(1)}, bf16[16,2,128,128]{3,2,1,0:T(8,128)(2,1)S(1)}, bf16[16,128,128]{2,1,0:T(8,128)(2,1)S(1)}, f32[16,8,128]{2,1,0:T(8,128)S(1)}) custom-call(bf16[128,2048]{1,0:T(8,128)(2,1)S(1)} %copy-done.4, bf16[128,2048]{1,0:T(8,128)(2,1)S(1)} %copy-done.5, ...), custom_call_target="tpu_custom_call" | custom-call | tf_op jit(solution)/shard_map/spread/pallas_call | solution.py:460
  59.8 0.0 copy-start.2
  59.8 1.0 copy-done.2
  60.8 0.0 copy-start.3
  60.8 1.0 copy-done.3
  61.8 0.0 copy-start.10
  61.8 0.8 copy-done.10
  62.6 0.0 copy-start.11
  62.6 0.8 copy-done.11
  63.4 0.0 copy-start.12
  63.4 0.6 copy-done.12
  64.0 30.3 %attend.1 = (bf16[2048,128]{1,0:T(8,128)(2,1)}, bf16[4096,128]{1,0:T(8,128)(2,1)}, bf16[4096,128]{1,0:T(8,128)(2,1)}) custom-call(s32[16]{0:T(128)} %docs_ref.1, bf16[2048,128]{1,0:T(8,128)(2,1)} %bitcast.12, bf16[4096,128]{1,0:T(8,128)(2,1)} %bitcast.9, bf16[4096,128]{1,0:T(8,128)(2,1)} %bitcast.10, bf16[2048,128]{1,0:T(8,128)(2,1)} %bitcast.13, ...), custom_call_target="tpu_custom_call" | custom-call | tf_op jit(solution)/shard_map/attend/pallas_call | solution.py:487
  94.3 0.0 copy-start
  94.3 1.2 copy-done
  95.5 0.0 copy-start.1
  95.5 1.2 copy-done.1
  96.7 0.0 copy-start.9
  96.7 1.0 copy-done.9
  97.8 40.1 %gather.1 = (bf16[128,2048]{1,0:T(8,128)(2,1)S(1)}, bf16[128,2048]{1,0:T(8,128)(2,1)S(1)}, bf16[128,2048]{1,0:T(8,128)(2,1)S(1)}) custom-call(bf16[16,128,128]{2,1,0:T(8,128)(2,1)S(1)} %bitcast.11, bf16[16,2,128,128]{3,2,1,0:T(8,128)(2,1)S(1)} %bitcast.7, bf16[16,2,128,128]{3,2,1,0:T(8,128)(2,1)S(1)} %bitcast.8), custom_call_target="tpu_custom_call" | custom-call | tf_op jit(solution)/shard_map/gather/pallas_call | solution.py:512
  137.9 0.8 copy.12
  138.7 0.8 copy.13
  139.5 0.8 copy.14
Async XLA Ops:
  0.6 1.0 copy-start.4
  1.7 1.0 copy-start.5
  2.7 1.0 copy-start.6
  3.8 1.0 copy-start.7
  4.8 1.0 copy-start.8
  59.8 1.0 copy-start.2
  60.8 1.0 copy-start.3
  61.8 0.8 copy-start.10
  62.6 0.8 copy-start.11
  63.4 0.6 copy-start.12
  94.3 1.2 copy-start
  95.5 1.2 copy-start.1
  96.7 1.0 copy-start.9

commit v2 on v1

v2 whole, which is shorter than its diff:
```python
import functools

import jax
import jax.numpy as jnp
from jax import lax
from jax.experimental import pallas as pl
from jax.experimental.pallas import tpu as pltpu
from jax.sharding import PartitionSpec as P

HEAD_DIM = 128
TILE = 512
BAND = 512
CHUNK = 512
PAIR = 2
NEG_FILL = -1e30
SCALE = HEAD_DIM ** (-0.5)
MESH = pl.DeviceIdType.MESH
NT = (((1,), (1,)), ((), ()))
NN = (((1,), (0,)), ((), ()))
TN = (((0,), (0,)), ((), ()))


def greet(groups, helpers, me, rep):
    barrier = pltpu.get_barrier_semaphore()

    def to_group(step, carry):
        pl.semaphore_signal(
            barrier, inc=1, device_id=(lax.rem(me + step, groups), rep), device_id_type=MESH
        )
        return carry

    lax.fori_loop(1, groups, to_group, 0)
    for step in range(1, helpers):
        pl.semaphore_signal(
            barrier, inc=1, device_id=(me, lax.rem(rep + step, helpers)), device_id_type=MESH
        )
    pl.semaphore_wait(barrier, groups - 1 + helpers - 1)


def windows(groups, helpers, tok):
    longest = max(tok * groups - TILE, BAND)

    def of(t, rep):
        first = (t * PAIR * helpers + rep) * tok
        last = ((t * PAIR + PAIR - 1) * helpers + rep) * tok + tok - 1
        lo = first - (longest - 1)
        if isinstance(lo, int):
            return max(lo, 0) // CHUNK, last // CHUNK + 1
        return jnp.maximum(lo, 0) // CHUNK, last // CHUNK + 1

    most = 0
    for t in range(groups // PAIR):
        for rep in range(helpers):
            lo, hi = of(t, rep)
            most = max(most, hi - lo)
    return of, most


def fused_kernel(
    groups,
    helpers,
    tok,
    keep,
    docs_ref,
    q_ref,
    k_ref,
    v_ref,
    o_ref,
    do_ref,
    gq,
    gk,
    gv,
    qr,
    kr,
    vr,
    dor,
    dlr,
    delta,
    stats,
    kept,
    dk_acc,
    dv_acc,
    mine_part,
    part,
    summed,
    dqs,
    send_sem,
    recv_sem,
    fsend_sem,
    frecv_sem,
    own_sem,
    hsend_sem,
    hrecv_sem,
    psend_sem,
    precv_sem,
    hown_sem,
):
    me = lax.axis_index("seq")
    rep = lax.axis_index("rep")
    width = PAIR * tok
    tiles = groups // PAIR
    blocks = CHUNK // tok
    window, most = windows(groups, helpers, tok)
    greet(groups, helpers, me, rep)

    def columns(ref, head):
        return ref.at[:, pl.ds(pl.multiple_of(head * HEAD_DIM, HEAD_DIM), HEAD_DIM)]

    def flat(s, r):
        return s * helpers + r

    K, Q, DO, V, DELTA = range(5)
    pairs = (
        (lambda g: columns(k_ref, g), lambda s: kr.at[flat(s, rep)]),
        (lambda g: columns(q_ref, g), lambda s: qr.at[s]),
        (lambda g: columns(do_ref, g), lambda s: dor.at[s]),
        (lambda g: columns(v_ref, g), lambda s: vr.at[flat(s, rep)]),
        (lambda g: delta.at[g], lambda s: dlr.at[s]),
    )

    def outgoing(which, step):
        to = lax.rem(me + step, groups)
        src, dst = pairs[which]
        return pltpu.make_async_remote_copy(
            src_ref=src(to),
            dst_ref=dst(me),
            send_sem=send_sem.at[which, step],
            recv_sem=recv_sem.at[which, step],
            device_id=(to, rep),
            device_id_type=MESH,
        )

    def arriving(which, step):
        source = lax.rem(me + groups - step, groups)
        src, dst = pairs[which]
        return pltpu.make_async_remote_copy(
            src_ref=src(source),
            dst_ref=dst(source),
            send_sem=send_sem.at[which, step],
            recv_sem=recv_sem.at[which, step],
            device_id=(source, rep),
            device_id_type=MESH,
        )

    def own(which):
        src, dst = pairs[which]
        return pltpu.make_async_copy(src(me), dst(me), own_sem.at[which])

    def forward(which, source, hop):
        ref = pairs[which][1](source)
        return pltpu.make_async_remote_copy(
            src_ref=ref,
            dst_ref=ref,
            send_sem=fsend_sem.at[which // V, hop - 1, source],
            recv_sem=frecv_sem.at[which // V, hop - 1, source],
            device_id=(me, lax.rem(rep + hop, helpers)),
            device_id_type=MESH,
        )

    def forwarded(which, source, hop):
        other = lax.rem(rep + helpers - hop, helpers)
        ref = (kr if which == K else vr).at[flat(source, other)]
        return pltpu.make_async_remote_copy(
            src_ref=ref,
            dst_ref=ref,
            send_sem=fsend_sem.at[which // V, hop - 1, source],
            recv_sem=frecv_sem.at[which // V, hop - 1, source],
            device_id=(me, other),
            device_id_type=MESH,
        )

    def send_all(which):
        own(which).start()

        def send(step, carry):
            outgoing(which, step).start()
            return carry

        lax.fori_loop(1, groups, send, 0)

    def take_all(which):
        own(which).wait()

        def take(step, carry):
            arriving(which, step).wait_recv()
            return carry

        lax.fori_loop(1, groups, take, 0)

    def relay(which, step):
        arriving(which, step).wait_recv()
        for hop in range(1, helpers):
            forward(which, lax.rem(me + groups - step, groups), hop).start()

    def relay_own(which):
        own(which).wait()
        for hop in range(1, helpers):
            forward(which, me, hop).start()

    def take_forwarded(which):
        def take(source, carry):
            for hop in range(1, helpers):
                forwarded(which, source, hop).wait_recv()
            return carry

        lax.fori_loop(0, groups, take, 0)

    for which in (K, Q, DO, V):
        send_all(which)

    def head_delta(head, carry):
        cols = pl.ds(pl.multiple_of(head * HEAD_DIM, HEAD_DIM), HEAD_DIM)
        prod = do_ref[:, cols].astype(jnp.float32) * o_ref[:, cols].astype(jnp.float32)
        row = jnp.sum(prod.T, axis=0, keepdims=True)
        delta[head] = jnp.broadcast_to(row, delta.shape[1:])
        return carry

    lax.fori_loop(0, groups, head_delta, 0)
    send_all(DELTA)

    def clear(b, carry):
        dk_acc[b] = jnp.zeros((tok, HEAD_DIM), jnp.float32)
        dv_acc[b] = jnp.zeros((tok, HEAD_DIM), jnp.float32)
        return carry

    lax.fori_loop(0, groups * helpers, clear, 0)

    def relay_step(which):
        def run(step, carry):
            relay(which, step)
            return carry

        return run

    relay_own(K)
    lax.fori_loop(1, groups, relay_step(K), 0)
    take_all(Q)
    take_forwarded(K)

    def chunk_of(ref, c):
        return ref[pl.ds(c * blocks, blocks)].reshape(CHUNK, HEAD_DIM)

    def rows_of(ref, t):
        return ref[pl.ds(t * PAIR, PAIR)].reshape(width, HEAD_DIM)

    def limits(t):
        lane = lax.broadcasted_iota(jnp.int32, (1, width), 1)
        row = ((t * PAIR + lane // tok) * helpers + rep) * tok + lane % tok

        def per_doc(d, state):
            end, starts = state
            end = end + docs_ref[d]
            return end, jnp.where(end <= row, end, starts)

        unused, starts = lax.fori_loop(
            0, docs_ref.shape[0], per_doc, (jnp.int32(0), jnp.zeros((1, width), jnp.int32))
        )
        return row, jnp.minimum(starts, row - (BAND - 1))

    def scores_of(c, queries, row, low):
        scores = lax.dot_general(
            chunk_of(kr, c), queries, NT, preferred_element_type=jnp.float32
        )
        kid = lax.broadcasted_iota(jnp.int32, (CHUNK, width), 0)
        allowed = (kid <= row - c * CHUNK) & (kid >= low - c * CHUNK)
        return jnp.where(allowed, scores * SCALE, NEG_FILL)

    def stat_tile(t, carry):
        lo, hi = window(t, rep)
        row, low = limits(t)
        queries = rows_of(qr, t)

        def stat(c, state):
            top, norm = state
            scores = scores_of(c, queries, row, low)
            if keep:
                kept[t * most + c - lo] = scores
            new_top = jnp.maximum(top, jnp.max(scores, axis=0, keepdims=True))
            fresh = jnp.sum(jnp.exp(scores - new_top), axis=0, keepdims=True)
            return new_top, norm * jnp.exp(top - new_top) + fresh

        start = (jnp.full((1, width), NEG_FILL, jnp.float32), jnp.zeros((1, width), jnp.float32))
        top, norm = lax.fori_loop(lo, hi, stat, start)
        stats[t] = jnp.broadcast_to(top + jnp.log(norm), stats.shape[1:])
        return carry

    lax.fori_loop(0, tiles, stat_tile, 0)
    take_all(DO)
    take_all(DELTA)
    relay_own(V)

    def value_tile(t, carry):
        for i in range(PAIR):
            step = t * PAIR + i

            @pl.when(step > 0)
            def _():
                relay(V, step)

        lo, hi = window(t, rep)
        douts = rows_of(dor, t)
        log_norm = stats[t, 0:1, :]
        if not keep:
            row, low = limits(t)
            queries = rows_of(qr, t)

        def value(c, carry):
            if keep:
                weights = jnp.exp(kept[t * most + c - lo] - log_norm)
                kept[t * most + c - lo] = weights
            else:
                weights = jnp.exp(scores_of(c, queries, row, low) - log_norm)
            add = lax.dot_general(
                weights.astype(jnp.bfloat16), douts, NN, preferred_element_type=jnp.float32
            )
            dv_acc[pl.ds(c * blocks, blocks)] += add.reshape(blocks, tok, HEAD_DIM)
            return carry

        lax.fori_loop(lo, hi, value, 0)
        return carry

    lax.fori_loop(0, tiles, value_tile, 0)

    results = (gk, gv, gq)

    def share(which, step, hop):
        to_rep = lax.rem(rep + hop, helpers)
        block = lax.rem(me + step, groups)
        return pltpu.make_async_remote_copy(
            src_ref=mine_part.at[which, flat(block, to_rep)],
            dst_ref=part.at[which, hop - 1, block],
            send_sem=psend_sem.at[which, hop - 1, step],
            recv_sem=precv_sem.at[which, hop - 1, step],
            device_id=(me, to_rep),
            device_id_type=MESH,
        )

    def source_of(which, block):
        return dqs.at[block] if which == 2 else summed.at[which, block]

    def home(which, step):
        to = lax.rem(me + step, groups)
        return pltpu.make_async_remote_copy(
            src_ref=source_of(which, to),
            dst_ref=columns(results[which], me),
            send_sem=hsend_sem.at[which, step],
            recv_sem=hrecv_sem.at[which, step],
            device_id=(to, rep),
            device_id_type=MESH,
        )

    def came(which, step):
        source = lax.rem(me + groups - step, groups)
        return pltpu.make_async_remote_copy(
            src_ref=source_of(which, source),
            dst_ref=columns(results[which], source),
            send_sem=hsend_sem.at[which, step],
            recv_sem=hrecv_sem.at[which, step],
            device_id=(source, rep),
            device_id_type=MESH,
        )

    def own_home(which):
        return pltpu.make_async_copy(
            source_of(which, me), columns(results[which], me), hown_sem.at[which]
        )

    accs = (dk_acc, dv_acc)
    factors = (SCALE, 1.0)

    def share_all(which):
        def run(step, carry):
            block = lax.rem(me + step, groups)
            for hop in range(1, helpers):
                at = flat(block, lax.rem(rep + hop, helpers))
                mine_part[which, at] = (accs[which][at] * factors[which]).astype(jnp.bfloat16)
                share(which, step, hop).start()
            return carry

        lax.fori_loop(0, groups, run, 0)

    def add(which, step):
        block = lax.rem(me + step, groups)
        value = accs[which][flat(block, rep)] * factors[which]
        for hop in range(1, helpers):
            share(which, step, hop).wait_recv()
            value = value + part[which, hop - 1, block].astype(jnp.float32)
        summed[which, block] = value.astype(jnp.bfloat16)

    def add_all(which):
        def run(step, carry):
            add(which, step)
            home(which, step).start()
            return carry

        add(which, 0)
        own_home(which).start()
        lax.fori_loop(1, groups, run, 0)

    share_all(1)
    take_forwarded(V)

    def grad_tile(turn, carry):
        t = lax.rem(turn + me // PAIR + 1, tiles)
        lo, hi = window(t, rep)
        queries = rows_of(qr, t)
        douts = rows_of(dor, t)
        log_norm = stats[t, 0:1, :]
        shift = jnp.concatenate([dlr[t * PAIR + i, 0:1, :] for i in range(PAIR)], axis=1)
        if not keep:
            row, low = limits(t)

        def grad(c, dq):
            if keep:
                weights = kept[t * most + c - lo]
            else:
                weights = jnp.exp(scores_of(c, queries, row, low) - log_norm)
            grad_weights = lax.dot_general(
                chunk_of(vr, c), douts, NT, preferred_element_type=jnp.float32
            )
            dscore = (weights * (grad_weights - shift)).astype(jnp.bfloat16)
            add = lax.dot_general(dscore, queries, NN, preferred_element_type=jnp.float32)
            dk_acc[pl.ds(c * blocks, blocks)] += add.reshape(blocks, tok, HEAD_DIM)
            return dq + lax.dot_general(
                chunk_of(kr, c), dscore, TN, preferred_element_type=jnp.float32
            )

        dq = lax.fori_loop(lo, hi, grad, jnp.zeros((HEAD_DIM, width), jnp.float32))
        rows = (dq.T * SCALE).astype(jnp.bfloat16)
        dqs[pl.ds(t * PAIR, PAIR)] = rows.reshape(PAIR, tok, HEAD_DIM)
        for i in range(PAIR):
            block = t * PAIR + i
            step = lax.rem(block + groups - me, groups)

            @pl.when(step > 0)
            def _():
                home(2, step).start()

        return carry

    lax.fori_loop(0, tiles // 2, grad_tile, 0)
    add_all(1)
    lax.fori_loop(tiles // 2, tiles, grad_tile, 0)
    share_all(0)
    own_home(2).start()
    add_all(0)

    for which in range(3):
        own_home(which).wait()

    def finish(step, carry):
        for which in range(5):
            outgoing(which, step).wait_send()
        for which in range(3):
            home(which, step).wait_send()
            came(which, step).wait_recv()
        return carry

    lax.fori_loop(1, groups, finish, 0)

    def finish_rep(step, carry):
        for hop in range(1, helpers):
            for which in (K, V):
                forward(which, step, hop).wait_send()
            for which in range(2):
                share(which, step, hop).wait_send()
        return carry

    lax.fori_loop(0, groups, finish_rep, 0)


def shards(queries, key_rows, value_rows, saved_output, grad_output, doc_lengths):
    groups = lax.axis_size("seq")
    helpers = lax.axis_size("rep")
    tok = queries.shape[0]
    everything = groups * helpers
    tiles = groups // PAIR
    low = jnp.bfloat16
    dma = pltpu.SemaphoreType.DMA
    vmem = pltpu.VMEM
    anywhere = pl.BlockSpec(memory_space=pl.ANY)
    in_vmem = pl.BlockSpec(memory_space=pltpu.VMEM)
    block = (tok, HEAD_DIM)
    unused, most = windows(groups, helpers, tok)
    slots = tiles * most
    keep = slots * CHUNK * PAIR * tok * 4 <= 24 << 20
    return pl.pallas_call(
        functools.partial(fused_kernel, groups, helpers, tok, keep),
        out_shape=(jax.ShapeDtypeStruct(queries.shape, low),) * 3,
        in_specs=[
            pl.BlockSpec(memory_space=pltpu.SMEM),
            anywhere,
            anywhere,
            anywhere,
            in_vmem,
            in_vmem,
        ],
        out_specs=[anywhere] * 3,
        scratch_shapes=[
            vmem((groups, *block), low),
            vmem((everything, *block), low),
            vmem((everything, *block), low),
            vmem((groups, *block), low),
            vmem((groups, 8, tok), jnp.float32),
            vmem((groups, 8, tok), jnp.float32),
            vmem((tiles, 8, PAIR * tok), jnp.float32),
            vmem((slots if keep else 1, CHUNK, PAIR * tok), jnp.float32),
            vmem((everything, *block), jnp.float32),
            vmem((everything, *block), jnp.float32),
            vmem((2, everything, *block), low),
            vmem((2, helpers - 1, groups, *block), low),
            vmem((2, groups, *block), low),
            vmem((groups, *block), low),
            dma((5, groups)),
            dma((5, groups)),
            dma((2, helpers - 1, groups)),
            dma((2, helpers - 1, groups)),
            dma((5,)),
            dma((3, groups)),
            dma((3, groups)),
            dma((2, helpers - 1, groups)),
            dma((2, helpers - 1, groups)),
            dma((3,)),
        ],
        compiler_params=pltpu.CompilerParams(
            collective_id=0, has_side_effects=True, vmem_limit_bytes=60 << 20
        ),
        name="fused",
    )(doc_lengths, queries, key_rows, value_rows, saved_output, grad_output)


def solution(mesh):
    tokens = P(("seq", "rep"), None)
    return jax.shard_map(
        shards,
        mesh=mesh,
        in_specs=(tokens,) * 5 + (P(),),
        out_specs=(tokens,) * 3,
        check_vma=False,
    )
```

time: 141 us -> 115 us (0.82)
  Pallas kernels: 124 us -> 110 us
  local copies, waits for them, and re-layouts: 15.2 us -> 3.97 us
    pallas_call x3 -> x1, Pallas kernels: 124 us -> 110 us  [shards(): pl.pallas_call(functools.partial(fused_kernel, groups, helpers, tok, keep...]
    unnamed x29 -> x7, local copies, waits for them, and re-layouts: 15.2 us -> 3.97 us
where the time goes in v2:
time: 115 us; the launch traced here: 114 us
  Pallas kernels  110 us (96%)
  local copies, waits for them, and re-layouts  3.97 us (3%)
    pallas_call x1, Pallas kernels, shards(): pl.pallas_call(functools.partial(fused_kernel, groups, helpers, tok, keep...  110 us
    unnamed x7, local copies, waits for them, and re-layouts  3.97 us

profile of v2, /device:TPU:13, one launch (start us, length us, event | category | flops | bytes accessed | tf_op | source)
XLA Modules:
  0.0 114.3 jit_solution(4193848267359832688)
XLA Ops:
  0.6 109.7 %fused.1 = (bf16[128,2048]{1,0:T(8,128)(2,1)}, bf16[128,2048]{1,0:T(8,128)(2,1)}, bf16[128,2048]{1,0:T(8,128)(2,1)}) custom-call(s32[16]{0:T(128)} %docs_ref.1, bf16[128,2048]{1,0:T(8,128)(2,1)} %q_ref.1, bf16[128,2048]{1,0:T(8,128)(2,1)} %k_ref.1, bf16[128,2048]{1,0:T(8,128)(2,1)} %v_ref.1, bf16[128,2048]{1,0:T(8,128)(2,1)} %o_ref.1, bf16[128,2048]{1,0:T(8,128)(2,1)} %do_ref.1), custom_call_target="tpu_custom_call" | custom-call | tf_op jit(solution)/shard_map/fused/pallas_call | solution.py:487
  110.3 0.0 copy-start.1
  110.3 1.9 %copy.12 = bf16[128,2048]{1,0:T(8,128)(2,1)} copy(bf16[128,2048]{1,0:T(8,128)(2,1)} %get-tuple-element.6) | data formatting | bytes 1048576
  112.3 0.0 copy-done.1
  112.3 0.0 copy-start
  112.3 0.8 copy.13
  113.1 0.4 copy-done
  113.5 0.8 copy.14
Async XLA Ops:
  110.3 2.0 %copy-start.1 = (bf16[128,2048]{1,0:T(8,128)(2,1)S(1)}, bf16[128,2048]{1,0:T(8,128)(2,1)}, u32[]{:S(2)}) copy-start(bf16[128,2048]{1,0:T(8,128)(2,1)} %get-tuple-element.7) | copy-start | bytes 1572868
  112.3 1.2 %copy-start = (bf16[128,2048]{1,0:T(8,128)(2,1)S(1)}, bf16[128,2048]{1,0:T(8,128)(2,1)}, u32[]{:S(2)}) copy-start(bf16[128,2048]{1,0:T(8,128)(2,1)} %get-tuple-element.8) | copy-start | bytes 1572868
